TPU v7x, 128 devices: a whole 4x4x4 slice. The times are simulated.
128 devices in a mesh: grp: 4 (over y), shard: 32 (over x, z, core).
Axes of the slice: x: 4, y: 4, z: 4, core: 2. Of those that a mesh axis runs over, the one named last changes fastest.
Arguments:
- new_rows: bfloat16 [32768, 1024], P(('grp', 'shard'))
- cluster_ids: int32 [32768], P(('grp', 'shard')), may hold values from 0 to 7, as said below
- new_order: int32 [32768], P(('grp', 'shard')), may hold values from 0 to 2147483646
- codes: bfloat16 [8, 8192, 1024], P('grp', 'shard'), may hold values from -8 to 8
- scales: float32 [8, 1024], P('grp')
- offsets: float32 [8, 1024], P('grp')
- counts: int32 [8], P('grp'), may hold values from 1024 to 8192, as said below
- earlier_order: int32 [8, 8192], P('grp', 'shard'), may hold values from 1 to 2147483646
Outputs:
- max_similarity: float32 [32768], P(('grp', 'shard'))
Inputs may be any that keep to these rules, and one draw needn't show every extreme that they name: `cluster_ids`: in each device's block of 256 rows, no group's clusters are named by more than 128 rows, and some group's clusters are named by exactly 128 rows. `counts`: some cluster has all 8192 slots live.
All inputs are finite; a program needn't handle non-finite values.
Results may differ from a plain program's by a relative error of at most 0.00047.
Values may be sent and summed in bfloat16 or wider, within the bound.
A program may use at most 128 MiB of HBM per device.

v0:
```python
import jax
import jax.numpy as jnp
from jax import lax
from jax.sharding import PartitionSpec as P

epsilon = 1e-06


def unit_rows(values):
    return (values / jnp.sqrt(jnp.sum(values * values, axis=-1, keepdims=True) + epsilon)).astype(
        jnp.bfloat16
    )


def score_clusters(
    running, queries, query_cluster, query_order, key_source, key_order, live_counts, prepare
):
    width = key_source.shape[1]
    positions = jnp.arange(width, dtype=jnp.int32)
    best = running
    for cluster in range(key_source.shape[0]):
        cluster_keys = prepare(key_source[cluster], cluster)
        scores = jnp.dot(queries, cluster_keys.T, preferred_element_type=jnp.float32)
        allowed = (
            (query_cluster[:, None] == cluster)
            & (positions[None, :] < live_counts[cluster])
            & (key_order[cluster][None, :] < query_order[:, None])
        )
        best = jnp.maximum(best, jnp.max(jnp.where(allowed, scores, -1.0), axis=1))
    return best


def per_device(new_rows, cluster_ids, new_order, codes, scales, offsets, counts, earlier_order):
    groups = lax.axis_size("grp")
    owned_count = codes.shape[0]
    local_rows = new_rows.shape[0]
    capacity = local_rows // 2
    queries = unit_rows(new_rows.astype(jnp.float32))
    target = cluster_ids // owned_count
    onehot = (target[:, None] == jnp.arange(groups, dtype=jnp.int32)[None, :]).astype(jnp.int32)
    slot_rank = jnp.sum((jnp.cumsum(onehot, axis=0) - onehot) * onehot, axis=1)
    position = target * capacity + slot_rank
    received = groups * capacity
    matches = position[None, :] == jnp.arange(received, dtype=jnp.int32)[:, None]
    filled = jnp.any(matches, axis=1)
    source_row = jnp.sum(
        jnp.where(matches, jnp.arange(local_rows, dtype=jnp.int32)[None, :], 0), axis=1
    )
    send_rows = jnp.take(queries, source_row, axis=0).reshape(groups, capacity, queries.shape[1])
    send_cluster = jnp.where(filled, jnp.take(cluster_ids % owned_count, source_row), 0).reshape(
        groups, capacity
    )
    send_order = jnp.where(filled, jnp.take(new_order, source_row), 0).reshape(groups, capacity)
    got_rows, got_cluster, got_order = (
        lax.all_to_all(send_rows, "grp", split_axis=0, concat_axis=0, tiled=True),
        lax.all_to_all(send_cluster, "grp", split_axis=0, concat_axis=0, tiled=True),
        lax.all_to_all(send_order, "grp", split_axis=0, concat_axis=0, tiled=True),
    )
    got_rows = got_rows.reshape(received, queries.shape[1])
    got_cluster = got_cluster.reshape(received)
    got_order = got_order.reshape(received)
    starting = jnp.zeros((received,), jnp.float32)

    def decode_one(code_rows, cluster):
        return unit_rows(
            code_rows.astype(jnp.float32) * scales[cluster][None, :] + offsets[cluster][None, :]
        )

    top_score = score_clusters(
        starting,
        got_rows,
        got_cluster,
        got_order,
        lax.all_gather(codes, "shard", axis=1, tiled=True),
        lax.all_gather(earlier_order, "shard", axis=1, tiled=True),
        counts,
        decode_one,
    )
    answered = lax.all_to_all(
        top_score.reshape(groups, capacity), "grp", split_axis=0, concat_axis=0, tiled=True
    )
    return jnp.take(answered.reshape(received), position)


def solution(mesh):
    return jax.shard_map(
        per_device,
        mesh=mesh,
        in_specs=(
            P(("grp", "shard"), None),
            P(("grp", "shard")),
            P(("grp", "shard")),
            P("grp", "shard", None),
            P("grp", None),
            P("grp", None),
            P("grp"),
            P("grp", "shard"),
        ),
        out_specs=P(("grp", "shard")),
        check_vma=False,
    )
```

profile of v0, /device:TPU:1, one launch (start us, length us, event | category | flops | bytes accessed | tf_op | source)
XLA Modules:
  0.0 194.6 jit_solution(17353483784496994221)
XLA Ops:
  6.5 0.7 all-gather.2.cloned.1.call-update
  7.3 0.7 and_select_fusion
  8.0 1.2 reduce-window.6
  10.3 3.5 %gather_fusion.2 = s32[512]{0:T(512)S(1)} fusion(s32[256]{0:T(256)S(1)} %get-tuple-element.20, s32[1024]{0:T(1024)S(1)} %pad_clamp_fusion.2), kind=kCustom, calls=%fused_computation.clone | custom fusion | bytes 6144 | tf_op jit(solution)/shard_map/jit(_take)/gather | solution.py:50
  13.9 3.5 %gather_fusion.3 = s32[512]{0:T(512)S(1)} fusion(s32[256]{0:T(256)S(1)} %copy-done, s32[1024]{0:T(1024)S(1)} %pad_clamp_fusion.2), kind=kCustom, calls=%fused_computation.1.clone | custom fusion | bytes 6144 | tf_op jit(solution)/shard_map/jit(_take)/gather | solution.py:53
  18.1 5.0 %all-to-all-start = ((s32[4,1,128]{2,1,0:T(1,128)}), s32[4,1,128]{2,1,0:T(1,128)S(1)}, u32[]{:S(2)}, u32[]{:S(2)}) async-start(s32[4,1,128]{2,1,0:T(1,128)} %bitcast.3), calls=%async_computation | async-start | bytes 4096 | tf_op jit(solution)/shard_map/all_to_all | solution.py:56
  23.1 1.3 fusion.26
  24.5 1.3 fusion.27
  25.8 2.1 %gather_fusion = bf16[512,1024]{1,0:T(8,128)(2,1)S(1)} fusion(bf16[256,1024]{1,0:T(8,128)(2,1)S(1)} %fusion.27, s32[1024]{0:T(1024)S(1)} %pad_clamp_fusion.1), kind=kCustom, calls=%fused_computation.2 | custom fusion | bytes 2099200 | tf_op jit(solution)/shard_map/jit(_take)/gather | solution.py:49
  27.9 26.3 %all_gather.6 = s32[2,8192]{1,0:T(2,128)S(1)} all-gather(s32[2,256]{1,0:T(2,128)} %param.17), channel_id=1, replica_groups=mesh['grp'=4,'shard'=32] {'shard'}, dimensions={1}, use_global_device_ids=true | all-gather | bytes 67584 | tf_op jit(solution)/shard_map/all_gather | solution.py:75
  54.1 1.3 fusion.35
  56.1 0.8 fusion.33
  56.9 0.8 fusion.34
  57.7 1.2 broadcast_select_fusion
  59.5 4.4 %all-to-all-start.1 = ((s32[4,1,128]{2,1,0:T(1,128)}), s32[4,1,128]{2,1,0:T(1,128)S(1)}, u32[]{:S(2)}, u32[]{:S(2)}) async-start(s32[4,1,128]{2,1,0:T(1,128)} %bitcast.6), calls=%async_computation.1 | async-start | bytes 4096 | tf_op jit(solution)/shard_map/all_to_all | solution.py:57
  64.0 4.0 %all-to-all-done.1 = s32[4,1,128]{2,1,0:T(1,128)S(1)} async-done(((s32[4,1,128]{2,1,0:T(1,128)}), s32[4,1,128]{2,1,0:T(1,128)S(1)}, u32[]{:S(2)}, u32[]{:S(2)}) %all-to-all-start.1) | async-done | bytes 2080 | tf_op jit(solution)/shard_map/all_to_all | solution.py:57
  68.0 3.5 %all-to-all-start.2 = ((bf16[4,128,1024]{2,1,0:T(8,128)(2,1)}), bf16[4,128,1024]{2,1,0:T(8,128)(2,1)S(1)}, u32[]{:S(2)}, u32[]{:S(2)}) async-start(bf16[4,128,1024]{2,1,0:T(8,128)(2,1)} %broadcast_select_fusion), calls=%async_computation.2 | async-start | bytes 2097152 | tf_op jit(solution)/shard_map/all_to_all | solution.py:55
  71.5 55.8 %all-gather.2.cloned.1.call-done = bf16[2,8192,1024]{2,1,0:T(8,128)(2,1)} async-done(((bf16[2,256,1024]{2,1,0:T(8,128)(2,1)}), bf16[2,8192,1024]{2,1,0:T(8,128)(2,1)}) %all-gather.2.cloned.1.call-update) | async-done | bytes 33554448 | tf_op jit(solution)/shard_map/all_gather | solution.py:74
  127.4 20.2 %fusion.6 = (f32[8192]{0:T(1024)S(1)}, f32[8192]{0:T(1024)S(1)}) fusion(f32[1024]{0:T(1024)S(1)} %bitcast.89, f32[1024]{0:T(1024)S(1)} %bitcast.87, bf16[2,8192,1024]{2,1,0:T(8,128)(2,1)} %all-gather.2.cloned.1.call-done, f32[1024]{0:T(1024)S(1)} %bitcast.85, f32[1024]{0:T(1024)S(1)} %bitcast.83), kind=kLoop, calls=%fused_computation.14 | loop fusion | flops 83869696 | bytes 33636352 | tf_op jit(solution)/shard_map/reduce_sum | solution.py:10
  147.6 14.4 %select_reduce_fusion.1 = f32[512]{0:T(512)S(1)} fusion(s32[8192]{0:T(1024)S(1)} %bitcast.81, s32[512]{0:T(512)S(1)} %bitcast.93, pred[8192]{0:T(1024)(128)(4,1)S(1)} %iota_compare_fusion.2, pred[512]{0:T(512)(128)(4,1)S(1)} %bitcast.96, bf16[512,1024]{1,0:T(8,128)(2,1)S(1)} %bitcast.77, f32[8192]{0:T(1024)S(1)} %get-tuple-element.25, ...), kind=kOutput, calls=%fused_computation.25 | convolution fusion | flops 8652849152 | bytes 17912320 | tf_op jit(solution)/shard_map/dot_general | solution.py:23
  162.0 14.5 %select_reduce_fusion = f32[512]{0:T(512)S(1)} fusion(s32[8192]{0:T(1024)S(1)} %bitcast.80, s32[512]{0:T(512)S(1)} %bitcast.94, pred[8192]{0:T(1024)(128)(4,1)S(1)} %iota_compare_fusion.1, pred[512]{0:T(512)(128)(4,1)S(1)} %bitcast.95, bf16[512,1024]{1,0:T(8,128)(2,1)S(1)} %bitcast.78, f32[8192]{0:T(1024)S(1)} %get-tuple-element.24, f32[1024]{0:T(1024)S(1)} %bitcast.86, ...), kind=kOutput, calls=%fused_computation.24 | convolution fusion | flops 8652849152 | bytes 17912320 | tf_op jit(solution)/shard_map/dot_general | solution.py:23
  177.1 4.0 %all-to-all-start.3 = ((f32[4,1,128]{2,1,0:T(1,128)}), f32[4,1,128]{2,1,0:T(1,128)S(1)}, u32[]{:S(2)}, u32[]{:S(2)}) async-start(f32[4,1,128]{2,1,0:T(1,128)} %bitcast.23), calls=%async_computation.3 | async-start | bytes 4096 | tf_op jit(solution)/shard_map/all_to_all | solution.py:79
  181.1 4.1 %all-to-all-done.3 = f32[4,1,128]{2,1,0:T(1,128)S(1)} async-done(((f32[4,1,128]{2,1,0:T(1,128)}), f32[4,1,128]{2,1,0:T(1,128)S(1)}, u32[]{:S(2)}, u32[]{:S(2)}) %all-to-all-start.3) | async-done | bytes 2080 | tf_op jit(solution)/shard_map/all_to_all | solution.py:79
  185.2 1.9 %gather_fusion.1 = f32[256]{0:T(256)S(1)} fusion(f32[512]{0:T(512)S(1)} %bitcast.75, s32[1024]{0:T(1024)S(1)} %pad_clamp_fusion), kind=kCustom, calls=%fused_computation.3 | custom fusion | bytes 3072 | tf_op jit(solution)/shard_map/jit(_take)/gather | solution.py:82
  (37 shorter events, 4.4 us)
Async XLA Ops:
  6.5 7.3 %copy-start = (s32[256]{0:T(256)S(1)}, s32[256]{0:T(256)}, u32[]{:S(2)}) copy-start(s32[256]{0:T(256)} %param.12) | copy-start | bytes 3076
  6.5 120.8 %all-gather.2.cloned.1.call-start = ((), (), s32[]{:S(2)}) async-start(), calls=%async_computation.4 | async-start | bytes 34603008 | tf_op jit(solution)/shard_map/all_gather | solution.py:74
  10.2 14.3 %copy-start.1 = (s32[256]{0:T(256)}, s32[256]{0:T(256)S(1)}, u32[]{:S(2)}) copy-start(s32[256]{0:T(256)S(1)} %get-tuple-element.11) | copy-start | bytes 3076
  18.1 41.4 %all-to-all-start = ((s32[4,1,128]{2,1,0:T(1,128)}), s32[4,1,128]{2,1,0:T(1,128)S(1)}, u32[]{:S(2)}, u32[]{:S(2)}) async-start(s32[4,1,128]{2,1,0:T(1,128)} %bitcast.3), calls=%async_computation | async-start | bytes 4096 | tf_op jit(solution)/shard_map/all_to_all | solution.py:56
  59.5 8.5 %all-to-all-start.1 = ((s32[4,1,128]{2,1,0:T(1,128)}), s32[4,1,128]{2,1,0:T(1,128)S(1)}, u32[]{:S(2)}, u32[]{:S(2)}) async-start(s32[4,1,128]{2,1,0:T(1,128)} %bitcast.6), calls=%async_computation.1 | async-start | bytes 4096 | tf_op jit(solution)/shard_map/all_to_all | solution.py:57
  68.0 79.6 %all-to-all-start.2 = ((bf16[4,128,1024]{2,1,0:T(8,128)(2,1)}), bf16[4,128,1024]{2,1,0:T(8,128)(2,1)S(1)}, u32[]{:S(2)}, u32[]{:S(2)}) async-start(bf16[4,128,1024]{2,1,0:T(8,128)(2,1)} %broadcast_select_fusion), calls=%async_computation.2 | async-start | bytes 2097152 | tf_op jit(solution)/shard_map/all_to_all | solution.py:55
  162.0 19.1 %copy-start.3 = (s32[256]{0:T(256)S(1)}, s32[256]{0:T(256)}, u32[]{:S(2)}) copy-start(s32[256]{0:T(256)} %get-tuple-element.10) | copy-start | bytes 3076
  162.0 25.1 %copy-start.2 = (s32[256]{0:T(256)S(1)}, s32[256]{0:T(256)}, u32[]{:S(2)}) copy-start(s32[256]{0:T(256)} %copy-done.1) | copy-start | bytes 3076
  177.1 8.1 %all-to-all-start.3 = ((f32[4,1,128]{2,1,0:T(1,128)}), f32[4,1,128]{2,1,0:T(1,128)S(1)}, u32[]{:S(2)}, u32[]{:S(2)}) async-start(f32[4,1,128]{2,1,0:T(1,128)} %bitcast.23), calls=%async_computation.3 | async-start | bytes 4096 | tf_op jit(solution)/shard_map/all_to_all | solution.py:79
Sparse Core Ops, SparseCore 0:
  9.7 117.5 all-gather.1
where the time goes:
time: 195 us
  waiting for transfers between devices  64.7 us (33%)
  other arithmetic  29.9 us (15%)
  matrix products  28.9 us (15%)
  blocking collectives  26.3 us (13%)
  starting transfers between devices  17 us (9%)
  local copies, waits for them, and re-layouts  14.3 us (7%)
  between operations  13.6 us (7%)
    all_gather x1, waiting for transfers between devices, per_device(): lax.all_gather(codes, 'shard', axis=1, tiled=True)  55.8 us
    dot_general x2, matrix products, score_clusters(): jnp.dot(queries, cluster_keys.T, preferred_element_type=jnp.float32)  28.9 us
    all_gather x1, blocking collectives, per_device(): lax.all_gather(earlier_order, 'shard', axis=1, tiled=True)  26.3 us
    reduce_sum x2, other arithmetic, unit_rows(): jnp.sum(values * values, axis=-1, keepdims=True) + epsilon  21.5 us
    all_to_all x1, starting transfers between devices, per_device(): lax.all_to_all(send_cluster, 'grp', split_axis=0, concat_axis=0, tiled=True)  5.01 us
    all_to_all x1, starting transfers between devices, per_device(): lax.all_to_all(send_order, 'grp', split_axis=0, concat_axis=0, tiled=True)  4.44 us
    all_to_all x1, waiting for transfers between devices, per_device(): lax.all_to_all(top_score.reshape(groups, capacity), 'grp', split_axis=0,...  4.1 us
    all_to_all x1, waiting for transfers between devices, per_device(): lax.all_to_all(send_order, 'grp', split_axis=0, concat_axis=0, tiled=True)  4.03 us
  transfers between devices with their start and end apart: 5, of which 3 were waited for; matrix products, arithmetic and copies ran while one was open for 21% of the time, Pallas kernels for 0%

commit v1 on v0

v1 whole, which is shorter than its diff:
```python
import functools

import jax
import jax.numpy as jnp
from jax import lax
from jax.experimental import pallas as pl
from jax.experimental.pallas import tpu as pltpu
from jax.sharding import PartitionSpec as P

MESH = pl.DeviceIdType.MESH
epsilon = 1e-06
DEAD = 2147483647
CH = 128

Q_ORDER = [
    (0, 0), (0, 3),
    (3, 0), (1, 0),
    (0, 1), (0, 2),
    (3, 3), (1, 3),
    (3, 1), (1, 1),
    (3, 2), (1, 2),
    (2, 0), (2, 3),
    (2, 1), (2, 2),
]
Q_SLOT = {place: i for i, place in enumerate(Q_ORDER)}
K_ORDER = [
    (0, 0, 0), (0, 0, 1), (0, 1, 0), (0, 1, 1),
    (0, 0, 2), (0, 0, 3), (0, 1, 2), (0, 1, 3),
]
J_ORDER = [0, 2, 1, 3]
for _j in J_ORDER:
    K_ORDER += [(3, 0, _j), (3, 1, _j), (1, 0, _j), (1, 1, _j)]
for _j in (0, 2):
    K_ORDER += [(2, 0, _j), (2, 1, _j), (2, 0, _j + 1), (2, 1, _j + 1)]
K_SLOT = {place: i for i, place in enumerate(K_ORDER)}
DY_ORDER = [0, 3, 1, 2]


def kernel(
    rows_hbm, ids_ref, order_ref, codes_hbm, scales_ref, offsets_ref, counts_ref, key_order_ref,
    out_ref,
    rows, codes, sendq, sendo, qbuf, kbuf, qord, kord, kob, acc, ans, perm,
    local_sem, send_sem, q_sem, k_sem, o_sem,
):
    y = lax.axis_index("grp")
    shard = lax.axis_index("shard")
    x, z, c = shard // 8, (shard // 2) % 4, shard % 2

    def device(dx=0, dy=0, dz=0, dc=0):
        return (
            (y + dy) % 4,
            (((x + dx) % 4) * 4 + (z + dz) % 4) * 2 + (c + dc) % 2,
        )

    started = []

    def send(src, dst, sem, to):
        copy = pltpu.make_async_remote_copy(
            src_ref=src,
            dst_ref=dst,
            send_sem=send_sem.at[len(started)],
            recv_sem=sem,
            device_id=to,
            device_id_type=MESH,
        )
        copy.start()
        started.append(copy)

    def arrived(dst, sem):
        pltpu.make_async_remote_copy(
            src_ref=dst,
            dst_ref=dst,
            send_sem=send_sem.at[0],
            recv_sem=sem,
            device_id=device(dc=1),
            device_id_type=MESH,
        ).wait_recv()

    def q_at(slot):
        return qbuf.at[pl.ds(slot * CH, CH), :]

    def k_at(slot):
        return kbuf.at[pl.ds(slot * CH, CH), :]

    rows_copy = pltpu.make_async_copy(rows_hbm, rows, local_sem.at[0])
    rows_copy.start()
    codes_copy = pltpu.make_async_copy(codes_hbm, codes, local_sem.at[1])
    codes_copy.start()
    barrier = pltpu.get_barrier_semaphore()
    line = [(dx, dy) for dx in range(4) for dy in range(4) if (dx, dy) != (0, 0)]
    column = [(dz, dc) for dz in range(4) for dc in range(2) if (dz, dc) != (0, 0)]
    for dx, dy in line:
        pl.semaphore_signal(barrier, inc=1, device_id=device(dx=dx, dy=dy), device_id_type=MESH)
    for dz, dc in column:
        pl.semaphore_signal(barrier, inc=1, device_id=device(dz=dz, dc=dc), device_id_type=MESH)

    n_rows = rows.shape[0]
    ids = ids_ref[...]
    target = (ids // 2 - y + 4) % 4
    groups = lax.broadcasted_iota(jnp.int32, (16, n_rows), 0)
    onehot = jnp.where(groups == target, 1.0, 0.0)
    before = lax.broadcasted_iota(jnp.int32, (n_rows, n_rows), 0) < lax.broadcasted_iota(
        jnp.int32, (n_rows, n_rows), 1
    )
    earlier = jnp.dot(
        onehot.astype(jnp.bfloat16),
        jnp.where(before, 1.0, 0.0).astype(jnp.bfloat16),
        preferred_element_type=jnp.float32,
    )
    position = jnp.sum(
        onehot * (earlier + (groups * CH).astype(jnp.float32)), axis=0, keepdims=True
    ).astype(jnp.int32)
    slots = lax.broadcasted_iota(jnp.int32, (4 * CH, n_rows), 0)
    perm[...] = jnp.where(slots == position, 1.0, 0.0).astype(jnp.bfloat16)

    order = order_ref[...]
    pieces = []
    for cluster in range(2):
        own = jnp.where(ids % 2 == cluster, order, 0)
        pieces += [(own >> (8 * p)) & 255 for p in range(4)]
    pieces = jnp.concatenate(pieces + pieces, axis=0).astype(jnp.float32).astype(jnp.bfloat16)
    moved = lax.dot_general(
        pieces, perm[...], (((1,), (1,)), ((), ())), preferred_element_type=jnp.float32
    ).astype(jnp.int32)
    for d in range(4):
        for cluster in range(2):
            part = moved[4 * cluster : 4 * cluster + 4, d * CH : (d + 1) * CH]
            joined = part[0:1] + part[1:2] * 256 + part[2:3] * 65536 + part[3:4] * 16777216
            if d == 0:
                qord[0, cluster : cluster + 1, :] = joined
            else:
                sendo[d, cluster : cluster + 1, :] = joined
    for j in range(4):
        place = shard * 256 + (j % 2) * CH + lax.broadcasted_iota(jnp.int32, (1, CH), 1)
        live = place < counts_ref[j // 2]
        kord[0, j : j + 1, :] = jnp.where(live, key_order_ref[j : j + 1, :], DEAD)

    rows_copy.wait()
    values = rows[...].astype(jnp.float32)
    queries = (
        values * lax.rsqrt(jnp.sum(values * values, axis=-1, keepdims=True) + epsilon)
    ).astype(jnp.bfloat16)

    def picked(d):
        return jnp.dot(
            perm[pl.ds(d * CH, CH), :], queries, preferred_element_type=jnp.float32
        ).astype(jnp.bfloat16)

    qbuf[pl.ds(0, CH), :] = picked(0)
    for d in range(1, 4):
        sendq[d] = picked(d)

    pl.semaphore_wait(barrier, len(line) + len(column))

    def send_x(dy):
        here = q_at(Q_SLOT[0, dy])
        for dx, there in ((1, 3), (3, 1)):
            slot = Q_SLOT[there, dy]
            send(here, q_at(slot), q_sem.at[slot], device(dx=dx))

    send_x(0)
    for d in (1, 3, 2):
        slot = Q_SLOT[0, (4 - d) % 4]
        send(sendq.at[d], q_at(slot), q_sem.at[slot], device(dy=d))

    codes_copy.wait()

    def spread(slot_of, j):
        here = k_at(slot_of(0, 0, j))
        for to, place in (
            (device(dz=1), (3, 0, j)),
            (device(dz=3), (1, 0, j)),
            (device(dc=1), (0, 1, j)),
        ):
            send(here, k_at(K_SLOT[place]), k_sem.at[K_SLOT[place]], to)

    for j in J_ORDER:
        decoded = (
            codes[pl.ds(j * CH, CH), :].astype(jnp.float32) * scales_ref[j // 2 : j // 2 + 1, :]
            + offsets_ref[j // 2 : j // 2 + 1, :]
        )
        kbuf[pl.ds(K_SLOT[0, 0, j] * CH, CH), :] = (
            decoded * lax.rsqrt(jnp.sum(decoded * decoded, axis=-1, keepdims=True) + epsilon)
        ).astype(jnp.bfloat16)
        spread(lambda *place: K_SLOT[place], j)

    for dz, dc in column:
        slot = dc * 4 + (4 - dz) % 4
        send(kord.at[0], kord.at[slot], o_sem.at[0], device(dz=dz, dc=dc))
    for dx, dy in line:
        slot = Q_SLOT[(4 - dx) % 4, (4 - dy) % 4]
        source = sendo.at[dy] if dy else qord.at[0]
        send(source, qord.at[slot], o_sem.at[1], device(dx=dx, dy=dy))

    acc[...] = jnp.zeros_like(acc)
    arrived(kord.at[pl.ds(1, 7)], o_sem.at[0])
    for slot, (dz, dc, j) in enumerate(K_ORDER):
        row = kord[dc * 4 + dz, j : j + 1, :]
        kob[pl.ds(slot * CH, CH), :] = jnp.broadcast_to(row, (CH, CH)).T
    arrived(qord.at[pl.ds(1, 15)], o_sem.at[1])

    def tile(kt, qt):
        keys = kbuf[pl.ds(pl.multiple_of(kt * 4 * CH, 4 * CH), 4 * CH), :]
        asks = qbuf[pl.ds(pl.multiple_of(qt * 2 * CH, 2 * CH), 2 * CH), :]
        return lax.dot_general(
            keys, asks, (((1,), (1,)), ((), ())), preferred_element_type=jnp.float32
        )

    def keep(kt, qt, scores):
        key_order = kob[pl.ds(pl.multiple_of(kt * 4 * CH, 4 * CH), 4 * CH), :]
        cluster = kt % 2
        for h in range(2):
            limit = qord[qt * 2 + h, pl.ds(cluster, 1), :]
            part = jnp.where(key_order < limit, scores[:, h * CH : (h + 1) * CH], 0.0)
            best = jnp.max(part.reshape(4 * CH // 8, 8, CH), axis=0)
            acc[qt * 2 + h] = jnp.maximum(acc[qt * 2 + h], best)

    def work(count, place):
        def pair(i, carry):
            first, second = place(2 * i), place(2 * i + 1)
            s0, s1 = tile(*first), tile(*second)
            keep(*first, s0)
            keep(*second, s1)
            return carry

        lax.fori_loop(0, count // 2, pair, 0)
        if count % 2:
            last = place(count - 1)
            keep(*last, tile(*last))

    def other_core(place):
        dz, _, j = place
        slot = K_SLOT[dz, 1, j]
        send(k_at(K_SLOT[place]), k_at(slot), k_sem.at[slot], device(dc=1))

    def got_keys(*places):
        for place in places:
            arrived(k_at(K_SLOT[place]), k_sem.at[K_SLOT[place]])

    def got_queries(*places):
        for place in places:
            arrived(q_at(Q_SLOT[place]), q_sem.at[Q_SLOT[place]])

    for tick in range(1, 7):
        if tick <= 4:
            j, dy = J_ORDER[tick - 1], DY_ORDER[tick - 1]
            for ready in {1: (3,), 2: (1, 2)}.get(tick, ()):
                got_queries((0, ready))
                send_x(ready)
            got_keys((3, 0, j), (1, 0, j))
            if j % 2 == 0:
                slot = K_SLOT[2, 0, j]
                send(k_at(K_SLOT[3, 0, j]), k_at(slot), k_sem.at[slot], device(dz=1))
            else:
                slot = K_SLOT[2, 0, j]
                send(k_at(K_SLOT[1, 0, j]), k_at(slot), k_sem.at[slot], device(dz=3))
            other_core((3, 0, j))
            other_core((1, 0, j))
            got_queries((3, dy), (1, dy))
            slot = Q_SLOT[2, dy]
            if dy in (0, 1):
                send(q_at(Q_SLOT[3, dy]), q_at(slot), q_sem.at[slot], device(dx=1))
            else:
                send(q_at(Q_SLOT[1, dy]), q_at(slot), q_sem.at[slot], device(dx=3))
            if tick == 1:
                got_keys(*((0, 1, own) for own in J_ORDER))
            got_keys((3, 1, j), (1, 1, j))
        else:
            j = 2 * (tick - 5)
            got_keys((2, 0, j), (2, 0, j + 1))
            other_core((2, 0, j))
            other_core((2, 0, j + 1))
            got_queries(*Q_ORDER[2 * tick + 2 : 2 * tick + 4])
            got_keys((2, 1, j), (2, 1, j + 1))
        if tick == 1:
            work(6, lambda i: (i % 3, i // 3))
        elif tick == 2:
            def place(i):
                late = i // 8
                return (i % 4) * (1 - late) + 3 * late, (2 + i // 4) * (1 - late) + (i - 8) * late

            work(10, place)
        else:

            def place(i, n=tick + 2):
                late = i // n
                return i * (1 - late) + (n - 1) * late, (n - 1) * (1 - late) + (i - n) * late

            work(2 * tick + 3, place)

    for dx, dy in line:
        slot = Q_SLOT[(4 - dx) % 4, (4 - dy) % 4]
        send(acc.at[Q_SLOT[dx, dy]], ans.at[slot], o_sem.at[2], device(dx=dx, dy=dy))
    arrived(ans.at[pl.ds(1, 15)], o_sem.at[2])
    answers = []
    for d in range(4):
        best = acc[0] if d == 0 else ans[Q_SLOT[0, d]]
        for dx in range(1, 4):
            best = jnp.maximum(best, ans[Q_SLOT[dx, d]])
        answers.append(jnp.max(best, axis=0, keepdims=True))
    answer = jnp.concatenate(answers, axis=1)
    high = answer.astype(jnp.bfloat16).astype(jnp.float32)
    middle = (answer - high).astype(jnp.bfloat16).astype(jnp.float32)
    low = answer - high - middle
    parts = jnp.concatenate([high, middle, low, jnp.zeros((13, 4 * CH), jnp.float32)], axis=0)
    back = jnp.dot(parts.astype(jnp.bfloat16), perm[...], preferred_element_type=jnp.float32)
    out_ref[...] = back[0:1] + back[1:2] + back[2:3]
    for copy in started:
        copy.wait_send()


def per_device(new_rows, cluster_ids, new_order, codes, scales, offsets, counts, earlier_order):
    n_rows, width = new_rows.shape
    vmem = pl.BlockSpec(memory_space=pltpu.VMEM)
    anywhere = pl.BlockSpec(memory_space=pl.ANY)
    smem = pl.BlockSpec(memory_space=pltpu.SMEM)
    n_q, n_k = len(Q_ORDER), len(K_ORDER)
    out = pl.pallas_call(
        kernel,
        out_shape=jax.ShapeDtypeStruct((1, n_rows), jnp.float32),
        in_specs=[anywhere, vmem, vmem, anywhere, vmem, vmem, smem, vmem],
        out_specs=vmem,
        scratch_shapes=[
            pltpu.VMEM((n_rows, width), jnp.bfloat16),
            pltpu.VMEM((4 * CH, width), jnp.bfloat16),
            pltpu.VMEM((4, CH, width), jnp.bfloat16),
            pltpu.VMEM((4, 2, CH), jnp.int32),
            pltpu.VMEM((n_q * CH, width), jnp.bfloat16),
            pltpu.VMEM((n_k * CH, width), jnp.bfloat16),
            pltpu.VMEM((n_q, 2, CH), jnp.int32),
            pltpu.VMEM((8, 4, CH), jnp.int32),
            pltpu.VMEM((n_k * CH, CH), jnp.int32),
            pltpu.VMEM((n_q, 8, CH), jnp.float32),
            pltpu.VMEM((n_q, 8, CH), jnp.float32),
            pltpu.VMEM((4 * CH, n_rows), jnp.bfloat16),
            pltpu.SemaphoreType.DMA((2,)),
            pltpu.SemaphoreType.DMA((96,)),
            pltpu.SemaphoreType.DMA((n_q,)),
            pltpu.SemaphoreType.DMA((n_k,)),
            pltpu.SemaphoreType.DMA((3,)),
        ],
        compiler_params=pltpu.CompilerParams(
            collective_id=0, has_side_effects=True, vmem_limit_bytes=48 * 2**20
        ),
        cost_estimate=pl.CostEstimate(
            flops=2 * n_q * n_k * CH * CH * width, bytes_accessed=2**21, transcendentals=1024
        ),
    )(
        new_rows,
        cluster_ids.reshape(1, n_rows),
        new_order.reshape(1, n_rows),
        codes.reshape(4 * CH, width),
        scales,
        offsets,
        counts,
        earlier_order.reshape(4, CH),
    )
    return out.reshape(n_rows)


def solution(mesh):
    return jax.shard_map(
        per_device,
        mesh=mesh,
        in_specs=(
            P(("grp", "shard"), None),
            P(("grp", "shard")),
            P(("grp", "shard")),
            P("grp", "shard", None),
            P("grp", None),
            P("grp", None),
            P("grp"),
            P("grp", "shard"),
        ),
        out_specs=P(("grp", "shard")),
        check_vma=False,
    )
```

time: 195 us -> 88.9 us (0.46)
  Pallas kernels: 0 us -> 83.5 us
  waiting for transfers between devices: 64.7 us -> 0 us
  other arithmetic: 29.9 us -> 0 us
  matrix products: 28.9 us -> 0 us
  blocking collectives: 26.3 us -> 0 us
  starting transfers between devices: 17 us -> 0 us
  between operations: 13.6 us -> 0.03 us
  local copies, waits for them, and re-layouts: 14.3 us -> 4.94 us
    pallas_call x0 -> x1, Pallas kernels: none -> 83.5 us  [per_device(): pl.pallas_call(kernel, out_shape=jax.ShapeDtypeStruct((1, n_rows), jnp.fl...]
    all_gather x1 -> x0, waiting for transfers between devices: 55.8 us -> none  [per_device(): lax.all_gather(codes, 'shard', axis=1, tiled=True)]
    dot_general x2 -> x0, matrix products: 28.9 us -> none  [score_clusters(): jnp.dot(queries, cluster_keys.T, preferred_element_type=jnp.float32)]
    all_gather x1 -> x0, blocking collectives: 26.3 us -> none  [per_device(): lax.all_gather(earlier_order, 'shard', axis=1, tiled=True)]
    reduce_sum x4 -> x0, other arithmetic: 21.6 us -> none  [the longest x2 21.5 us: unit_rows(): jnp.sum(values * values, axis=-1, keepdims=True) + epsilon]
    all_to_all x4 -> x0, starting transfers between devices: 17 us -> none  [the longest x1 5.01 us: per_device(): lax.all_to_all(send_cluster, 'grp', split_axis=0, concat_axis=0, tiled=True)]
    gather x4 -> x0, local copies, waits for them, and re-layouts: 11 us -> none  [the longest x1 3.52 us: per_device(): jnp.take(cluster_ids % owned_count, source_row)]
    all_to_all x4 -> x0, waiting for transfers between devices: 8.13 us -> none  [the longest x1 4.1 us: per_device(): lax.all_to_all(top_score.reshape(groups, capacity), 'grp', split_axis=0,...]
  transfers between devices with their start and end apart: 5 -> 0, of which waited for: 3 -> 0; matrix products, arithmetic and copies ran while one was open for 21% -> 0% of each run, Pallas kernels for 0% -> 0%
where the time goes in v1:
time: 88.9 us; the launch traced here: 88.4 us
  Pallas kernels  83.5 us (94%)
  local copies, waits for them, and re-layouts  4.94 us (6%)
    pallas_call x1, Pallas kernels, per_device(): pl.pallas_call(kernel, out_shape=jax.ShapeDtypeStruct((1, n_rows), jnp.fl...  83.5 us
    unnamed x15, local copies, waits for them, and re-layouts  4.21 us

profile of v1, /device:TPU:1, one launch (start us, length us, event | category | flops | bytes accessed | tf_op | source)
XLA Modules:
  0.0 88.4 jit_solution(15501518811339175195)
XLA Ops:
  0.0 0.0 copy-start.2
  0.0 0.0 copy-start.4
  0.0 0.0 copy-start.6
  0.0 0.7 reshape.18.key_order_ref
  0.7 0.0 copy-done.2
  0.7 0.0 copy-done.4
  0.7 0.0 copy-done.6
  0.8 0.0 copy-start
  0.8 1.2 %copy-done = bf16[2,256,1024]{2,1,0:T(8,128)(2,1)S(1)} copy-done((bf16[2,256,1024]{2,1,0:T(8,128)(2,1)S(1)}, bf16[2,256,1024]{2,1,0:T(8,128)(2,1)}, u32[]{:S(2)}) %copy-start) | copy-done | bytes 1048600
  2.0 0.0 copy-start.1
  2.0 1.0 %copy-done.1 = bf16[256,1024]{1,0:T(8,128)(2,1)S(1)} copy-done((bf16[256,1024]{1,0:T(8,128)(2,1)S(1)}, bf16[256,1024]{1,0:T(8,128)(2,1)}, u32[]{:S(2)}) %copy-start.1) | copy-done | bytes 524312
  3.0 0.0 copy-start.3
  3.0 0.7 copy-done.3
  3.7 0.0 copy-start.5
  3.7 0.7 copy-done.5
  4.4 83.5 %shard_map.82 = f32[1,256]{1,0:T(1,128)S(1)} custom-call(bf16[256,1024]{1,0:T(8,128)(2,1)S(1)} %copy-done.1, s32[1,256]{1,0:T(1,128)S(1)} %bitcast.6, s32[1,256]{1,0:T(1,128)S(1)} %bitcast.7, bf16[512,1024]{1,0:T(8,128)(2,1)S(1)} %bitcast.5, f32[2,1024]{1,0:T(2,128)S(1)} %copy-done.2, f32[2,1024]{1,0:T(2,128)S(1)} %copy-done.3, s32[2]{0:T(128)S(1)} %copy-done.6, ...), custom_call_target="tpu_custom_call" | custom-call | flops 17179869184 | bytes 2097152 | tf_op jit(solution)/shard_map/pallas_call | solution.py:318
  87.9 0.6 copy.10
Async XLA Ops:
  0.0 0.7 copy-start.2
  0.0 0.7 copy-start.4
  0.0 0.7 copy-start.6
  0.8 1.2 %copy-start = (bf16[2,256,1024]{2,1,0:T(8,128)(2,1)S(1)}, bf16[2,256,1024]{2,1,0:T(8,128)(2,1)}, u32[]{:S(2)}) copy-start(bf16[2,256,1024]{2,1,0:T(8,128)(2,1)} %param.11) | copy-start | bytes 3145732
  2.0 1.0 %copy-start.1 = (bf16[256,1024]{1,0:T(8,128)(2,1)S(1)}, bf16[256,1024]{1,0:T(8,128)(2,1)}, u32[]{:S(2)}) copy-start(bf16[256,1024]{1,0:T(8,128)(2,1)} %rows_hbm.1) | copy-start | bytes 1572868
  3.0 0.7 copy-start.3
  3.7 0.7 copy-start.5

commit v2 on v1

--- a/solution.py
+++ b/solution.py
@@ -37,9 +37,10 @@
 
 
 def kernel(
-    rows_hbm, ids_ref, order_ref, codes_hbm, scales_ref, offsets_ref, counts_ref, key_order_ref,
+    rows_hbm, ids_hbm, order_hbm, codes_hbm, scales_hbm, offsets_hbm, counts_hbm, key_order_hbm,
     out_ref,
-    rows, codes, sendq, sendo, qbuf, kbuf, qord, kord, kob, acc, ans, perm,
+    rows, ids_ref, order_ref, codes, scales_ref, offsets_ref, counts_ref, key_order_ref,
+    sendq, sendo, qbuf, kbuf, qord, kord, kob, acc, ans, perm,
     local_sem, send_sem, q_sem, k_sem, o_sem,
 ):
     y = lax.axis_index("grp")
@@ -82,10 +83,23 @@
     def k_at(slot):
         return kbuf.at[pl.ds(slot * CH, CH), :]
 
-    rows_copy = pltpu.make_async_copy(rows_hbm, rows, local_sem.at[0])
-    rows_copy.start()
-    codes_copy = pltpu.make_async_copy(codes_hbm, codes, local_sem.at[1])
-    codes_copy.start()
+    loads = [
+        pltpu.make_async_copy(src, dst, local_sem.at[i])
+        for i, (src, dst) in enumerate(
+            (
+                (ids_hbm, ids_ref),
+                (order_hbm, order_ref),
+                (counts_hbm, counts_ref),
+                (key_order_hbm, key_order_ref),
+                (rows_hbm, rows),
+                (scales_hbm, scales_ref),
+                (offsets_hbm, offsets_ref),
+                (codes_hbm, codes),
+            )
+        )
+    ]
+    for load in loads:
+        load.start()
     barrier = pltpu.get_barrier_semaphore()
     line = [(dx, dy) for dx in range(4) for dy in range(4) if (dx, dy) != (0, 0)]
     column = [(dz, dc) for dz in range(4) for dc in range(2) if (dz, dc) != (0, 0)]
@@ -95,6 +109,8 @@
         pl.semaphore_signal(barrier, inc=1, device_id=device(dz=dz, dc=dc), device_id_type=MESH)
 
     n_rows = rows.shape[0]
+    for load in loads[:4]:
+        load.wait()
     ids = ids_ref[...]
     target = (ids // 2 - y + 4) % 4
     groups = lax.broadcasted_iota(jnp.int32, (16, n_rows), 0)
@@ -133,9 +149,11 @@
     for j in range(4):
         place = shard * 256 + (j % 2) * CH + lax.broadcasted_iota(jnp.int32, (1, CH), 1)
         live = place < counts_ref[j // 2]
-        kord[0, j : j + 1, :] = jnp.where(live, key_order_ref[j : j + 1, :], DEAD)
-
-    rows_copy.wait()
+        kord[0, j : j + 1, :] = jnp.where(
+            live, key_order_ref[j // 2 : j // 2 + 1, (j % 2) * CH : (j % 2 + 1) * CH], DEAD
+        )
+
+    loads[4].wait()
     values = rows[...].astype(jnp.float32)
     queries = (
         values * lax.rsqrt(jnp.sum(values * values, axis=-1, keepdims=True) + epsilon)
@@ -158,12 +176,21 @@
             slot = Q_SLOT[there, dy]
             send(here, q_at(slot), q_sem.at[slot], device(dx=dx))
 
+    for dz, dc in column:
+        slot = dc * 4 + (4 - dz) % 4
+        send(kord.at[0], kord.at[slot], o_sem.at[0], device(dz=dz, dc=dc))
+    for dx, dy in line:
+        slot = Q_SLOT[(4 - dx) % 4, (4 - dy) % 4]
+        source = sendo.at[dy] if dy else qord.at[0]
+        send(source, qord.at[slot], o_sem.at[1], device(dx=dx, dy=dy))
+
     send_x(0)
     for d in (1, 3, 2):
         slot = Q_SLOT[0, (4 - d) % 4]
         send(sendq.at[d], q_at(slot), q_sem.at[slot], device(dy=d))
 
-    codes_copy.wait()
+    for load in loads[5:]:
+        load.wait()
 
     def spread(slot_of, j):
         here = k_at(slot_of(0, 0, j))
@@ -184,14 +211,6 @@
         ).astype(jnp.bfloat16)
         spread(lambda *place: K_SLOT[place], j)
 
-    for dz, dc in column:
-        slot = dc * 4 + (4 - dz) % 4
-        send(kord.at[0], kord.at[slot], o_sem.at[0], device(dz=dz, dc=dc))
-    for dx, dy in line:
-        slot = Q_SLOT[(4 - dx) % 4, (4 - dy) % 4]
-        source = sendo.at[dy] if dy else qord.at[0]
-        send(source, qord.at[slot], o_sem.at[1], device(dx=dx, dy=dy))
-
     acc[...] = jnp.zeros_like(acc)
     arrived(kord.at[pl.ds(1, 7)], o_sem.at[0])
     for slot, (dz, dc, j) in enumerate(K_ORDER):
@@ -199,34 +218,46 @@
         kob[pl.ds(slot * CH, CH), :] = jnp.broadcast_to(row, (CH, CH)).T
     arrived(qord.at[pl.ds(1, 15)], o_sem.at[1])
 
-    def tile(kt, qt):
-        keys = kbuf[pl.ds(pl.multiple_of(kt * 4 * CH, 4 * CH), 4 * CH), :]
-        asks = qbuf[pl.ds(pl.multiple_of(qt * 2 * CH, 2 * CH), 2 * CH), :]
+    def tile(key_row, n_keys, block, n_blocks):
+        keys = kbuf[pl.ds(pl.multiple_of(key_row, 2 * CH), n_keys), :]
+        asks = qbuf[pl.ds(pl.multiple_of(block * CH, CH), n_blocks * CH), :]
         return lax.dot_general(
             keys, asks, (((1,), (1,)), ((), ())), preferred_element_type=jnp.float32
         )
 
-    def keep(kt, qt, scores):
-        key_order = kob[pl.ds(pl.multiple_of(kt * 4 * CH, 4 * CH), 4 * CH), :]
-        cluster = kt % 2
-        for h in range(2):
-            limit = qord[qt * 2 + h, pl.ds(cluster, 1), :]
+    def keep(key_row, n_keys, block, n_blocks, scores):
+        key_order = kob[pl.ds(pl.multiple_of(key_row, 2 * CH), n_keys), :]
+        cluster = (key_row // (4 * CH)) % 2
+        for h in range(n_blocks):
+            limit = qord[block + h, pl.ds(cluster, 1), :]
             part = jnp.where(key_order < limit, scores[:, h * CH : (h + 1) * CH], 0.0)
-            best = jnp.max(part.reshape(4 * CH // 8, 8, CH), axis=0)
-            acc[qt * 2 + h] = jnp.maximum(acc[qt * 2 + h], best)
-
-    def work(count, place):
-        def pair(i, carry):
-            first, second = place(2 * i), place(2 * i + 1)
-            s0, s1 = tile(*first), tile(*second)
-            keep(*first, s0)
-            keep(*second, s1)
+            best = jnp.max(part.reshape(n_keys // 8, 8, CH), axis=0)
+            acc[block + h] = jnp.maximum(acc[block + h], best)
+
+    def work(count, place, n_keys, n_blocks, together):
+        def some(first, size):
+            at = [place(first + i) for i in range(size)]
+            scores = [tile(row, n_keys, block, n_blocks) for row, block in at]
+            for (row, block), found in zip(at, scores):
+                keep(row, n_keys, block, n_blocks, found)
+
+        def step(i, carry):
+            some(together * i, together)
             return carry
 
-        lax.fori_loop(0, count // 2, pair, 0)
-        if count % 2:
-            last = place(count - 1)
-            keep(*last, tile(*last))
+        lax.fori_loop(0, count // together, step, 0)
+        if count % together:
+            some(count - count % together, count % together)
+
+    def new_queries(qt, n_qt, n_kt):
+        work(
+            n_kt * n_qt, lambda i: ((i % n_kt) * 4 * CH, (qt + i // n_kt) * 2), 4 * CH, 2, 2
+        )
+
+    def new_keys(kt, n_qt):
+        work(n_qt // 2, lambda i: (kt * 4 * CH, i * 4), 4 * CH, 4, 1)
+        if n_qt % 2:
+            work(1, lambda i: (kt * 4 * CH, (n_qt - 1) * 2), 4 * CH, 2, 1)
 
     def other_core(place):
         dz, _, j = place
@@ -248,11 +279,10 @@
                 got_queries((0, ready))
                 send_x(ready)
             got_keys((3, 0, j), (1, 0, j))
+            slot = K_SLOT[2, 0, j]
             if j % 2 == 0:
-                slot = K_SLOT[2, 0, j]
                 send(k_at(K_SLOT[3, 0, j]), k_at(slot), k_sem.at[slot], device(dz=1))
             else:
-                slot = K_SLOT[2, 0, j]
                 send(k_at(K_SLOT[1, 0, j]), k_at(slot), k_sem.at[slot], device(dz=3))
             other_core((3, 0, j))
             other_core((1, 0, j))
@@ -264,29 +294,28 @@
                 send(q_at(Q_SLOT[1, dy]), q_at(slot), q_sem.at[slot], device(dx=3))
             if tick == 1:
                 got_keys(*((0, 1, own) for own in J_ORDER))
+                new_queries(0, 2, 2)
+                n_q = 2
+            elif tick == 2:
+                new_queries(2, 2, 3)
+                n_q = 4
+            else:
+                new_queries(tick + 1, 1, tick + 1)
+                n_q = tick + 2
             got_keys((3, 1, j), (1, 1, j))
+            new_keys(tick + 1, n_q)
         else:
             j = 2 * (tick - 5)
+            got_queries(*Q_ORDER[2 * tick + 2 : 2 * tick + 4])
+            if tick == 6:
+                new_queries(7, 1, 7)
             got_keys((2, 0, j), (2, 0, j + 1))
             other_core((2, 0, j))
             other_core((2, 0, j + 1))
-            got_queries(*Q_ORDER[2 * tick + 2 : 2 * tick + 4])
+            if tick == 5:
+                new_queries(6, 1, 6)
             got_keys((2, 1, j), (2, 1, j + 1))
-        if tick == 1:
-            work(6, lambda i: (i % 3, i // 3))
-        elif tick == 2:
-            def place(i):
-                late = i // 8
-                return (i % 4) * (1 - late) + 3 * late, (2 + i // 4) * (1 - late) + (i - 8) * late
-
-            work(10, place)
-        else:
-
-            def place(i, n=tick + 2):
-                late = i // n
-                return i * (1 - late) + (n - 1) * late, (n - 1) * (1 - late) + (i - n) * late
-
-            work(2 * tick + 3, place)
+            new_keys(tick + 1, tick + 2)
 
     for dx, dy in line:
         slot = Q_SLOT[(4 - dx) % 4, (4 - dy) % 4]
@@ -312,17 +341,21 @@
 def per_device(new_rows, cluster_ids, new_order, codes, scales, offsets, counts, earlier_order):
     n_rows, width = new_rows.shape
     vmem = pl.BlockSpec(memory_space=pltpu.VMEM)
-    anywhere = pl.BlockSpec(memory_space=pl.ANY)
-    smem = pl.BlockSpec(memory_space=pltpu.SMEM)
     n_q, n_k = len(Q_ORDER), len(K_ORDER)
     out = pl.pallas_call(
         kernel,
         out_shape=jax.ShapeDtypeStruct((1, n_rows), jnp.float32),
-        in_specs=[anywhere, vmem, vmem, anywhere, vmem, vmem, smem, vmem],
+        in_specs=[pl.BlockSpec(memory_space=pl.ANY)] * 8,
         out_specs=vmem,
         scratch_shapes=[
             pltpu.VMEM((n_rows, width), jnp.bfloat16),
+            pltpu.VMEM((1, n_rows), jnp.int32),
+            pltpu.VMEM((1, n_rows), jnp.int32),
             pltpu.VMEM((4 * CH, width), jnp.bfloat16),
+            pltpu.VMEM((2, width), jnp.float32),
+            pltpu.VMEM((2, width), jnp.float32),
+            pltpu.SMEM((2,), jnp.int32),
+            pltpu.VMEM((2, 2 * CH), jnp.int32),
             pltpu.VMEM((4, CH, width), jnp.bfloat16),
             pltpu.VMEM((4, 2, CH), jnp.int32),
             pltpu.VMEM((n_q * CH, width), jnp.bfloat16),
@@ -333,14 +366,14 @@
             pltpu.VMEM((n_q, 8, CH), jnp.float32),
             pltpu.VMEM((n_q, 8, CH), jnp.float32),
             pltpu.VMEM((4 * CH, n_rows), jnp.bfloat16),
-            pltpu.SemaphoreType.DMA((2,)),
+            pltpu.SemaphoreType.DMA((8,)),
             pltpu.SemaphoreType.DMA((96,)),
             pltpu.SemaphoreType.DMA((n_q,)),
             pltpu.SemaphoreType.DMA((n_k,)),
             pltpu.SemaphoreType.DMA((3,)),
         ],
         compiler_params=pltpu.CompilerParams(
-            collective_id=0, has_side_effects=True, vmem_limit_bytes=48 * 2**20
+            collective_id=0, has_side_effects=True, vmem_limit_bytes=63 * 2**20
         ),
         cost_estimate=pl.CostEstimate(
             flops=2 * n_q * n_k * CH * CH * width, bytes_accessed=2**21, transcendentals=1024
@@ -353,7 +386,7 @@
         scales,
         offsets,
         counts,
-        earlier_order.reshape(4, CH),
+        earlier_order,
     )
     return out.reshape(n_rows)
 

time: 88.9 us -> 65.5 us (0.74)
  Pallas kernels: 83.5 us -> 64.1 us
  local copies, waits for them, and re-layouts: 4.94 us -> 1.22 us
    pallas_call x1, Pallas kernels: 83.5 us -> 64.1 us  [per_device(): pl.pallas_call(kernel, out_shape=jax.ShapeDtypeStruct((1, n_rows), jnp.fl...]
    unnamed x15 -> x3, local copies, waits for them, and re-layouts: 4.21 us -> 1.22 us
where the time goes in v2:
time: 65.5 us; the launch traced here: 65.4 us
  Pallas kernels  64.1 us (98%)
  local copies, waits for them, and re-layouts  1.22 us (2%)
    pallas_call x1, Pallas kernels, per_device(): pl.pallas_call(kernel, out_shape=jax.ShapeDtypeStruct((1, n_rows), jnp.fl...  64.1 us

profile of v2, /device:TPU:1, one launch (start us, length us, event | category | flops | bytes accessed | tf_op | source)
XLA Modules:
  0.0 65.4 jit_solution(14659515318193229132)
XLA Ops:
  0.0 64.1 %shard_map.82 = f32[1,256]{1,0:T(1,128)} custom-call(bf16[256,1024]{1,0:T(8,128)(2,1)} %rows_hbm.1, s32[1,256]{1,0:T(1,128)} %bitcast.6, s32[1,256]{1,0:T(1,128)} %bitcast.7, bf16[512,1024]{1,0:T(8,128)(2,1)} %bitcast.5, f32[2,1024]{1,0:T(2,128)} %scales_hbm.1, f32[2,1024]{1,0:T(2,128)} %offsets_hbm.1, s32[2]{0:T(128)} %counts_hbm.1, s32[2,256]{1,0:T(2,128)} %key_order_hbm.1), custom_call_target="tpu_custom_call" | custom-call | flops 17179869184 | bytes 2097152 | tf_op jit(solution)/shard_map/pallas_call | solution.py:345
  64.2 0.0 copy-start
  64.2 0.7 copy-done
  64.8 0.6 copy.10
Async XLA Ops:
  64.2 0.7 %copy-start = (f32[1,256]{1,0:T(1,128)S(1)}, f32[1,256]{1,0:T(1,128)}, u32[]{:S(2)}) copy-start(f32[1,256]{1,0:T(1,128)} %shard_map.82) | copy-start | bytes 3076

commit v3 on v2

--- a/solution.py
+++ b/solution.py
@@ -11,6 +11,7 @@
 epsilon = 1e-06
 DEAD = 2147483647
 CH = 128
+HALF = CH // 2
 
 Q_ORDER = [
     (0, 0), (0, 3),
@@ -32,7 +33,11 @@
     K_ORDER += [(3, 0, _j), (3, 1, _j), (1, 0, _j), (1, 1, _j)]
 for _j in (0, 2):
     K_ORDER += [(2, 0, _j), (2, 1, _j), (2, 0, _j + 1), (2, 1, _j + 1)]
-K_SLOT = {place: i for i, place in enumerate(K_ORDER)}
+K_ROW = {
+    place + (h,): i * CH + h * HALF if i < 28 else 28 * CH + h * 4 * HALF + (i - 28) * HALF
+    for i, place in enumerate(K_ORDER)
+    for h in range(2)
+}
 DY_ORDER = [0, 3, 1, 2]
 
 
@@ -77,11 +82,13 @@
             device_id_type=MESH,
         ).wait_recv()
 
-    def q_at(slot):
-        return qbuf.at[pl.ds(slot * CH, CH), :]
-
-    def k_at(slot):
-        return kbuf.at[pl.ds(slot * CH, CH), :]
+    def q_half(place, h):
+        slot = Q_SLOT[place]
+        return qbuf.at[pl.ds(slot * CH + h * HALF, HALF), :], q_sem.at[2 * slot + h]
+
+    def k_part(place, h=None):
+        row = K_ROW[place + (h or 0,)]
+        return kbuf.at[pl.ds(row, CH if h is None else HALF), :], k_sem.at[row // HALF]
 
     loads = [
         pltpu.make_async_copy(src, dst, local_sem.at[i])
@@ -170,11 +177,13 @@
 
     pl.semaphore_wait(barrier, len(line) + len(column))
 
-    def send_x(dy):
-        here = q_at(Q_SLOT[0, dy])
+    def send_x(dy, h):
+        here, _ = q_half((0, dy), h)
         for dx, there in ((1, 3), (3, 1)):
-            slot = Q_SLOT[there, dy]
-            send(here, q_at(slot), q_sem.at[slot], device(dx=dx))
+            send(here, *q_half((there, dy), h), device(dx=dx))
+
+    def send_y(d, h):
+        send(sendq.at[d, pl.ds(h * HALF, HALF)], *q_half((0, (4 - d) % 4), h), device(dy=d))
 
     for dz, dc in column:
         slot = dc * 4 + (4 - dz) % 4
@@ -184,38 +193,39 @@
         source = sendo.at[dy] if dy else qord.at[0]
         send(source, qord.at[slot], o_sem.at[1], device(dx=dx, dy=dy))
 
-    send_x(0)
-    for d in (1, 3, 2):
-        slot = Q_SLOT[0, (4 - d) % 4]
-        send(sendq.at[d], q_at(slot), q_sem.at[slot], device(dy=d))
+    for h in range(2):
+        for d in (1, 3):
+            send_y(d, h)
+        send_x(0, h)
 
     for load in loads[5:]:
         load.wait()
 
-    def spread(slot_of, j):
-        here = k_at(slot_of(0, 0, j))
+    def spread(j):
+        here, _ = k_part((0, 0, j))
         for to, place in (
             (device(dz=1), (3, 0, j)),
             (device(dz=3), (1, 0, j)),
             (device(dc=1), (0, 1, j)),
         ):
-            send(here, k_at(K_SLOT[place]), k_sem.at[K_SLOT[place]], to)
+            send(here, *k_part(place), to)
 
     for j in J_ORDER:
         decoded = (
             codes[pl.ds(j * CH, CH), :].astype(jnp.float32) * scales_ref[j // 2 : j // 2 + 1, :]
             + offsets_ref[j // 2 : j // 2 + 1, :]
         )
-        kbuf[pl.ds(K_SLOT[0, 0, j] * CH, CH), :] = (
+        kbuf[pl.ds(K_ROW[0, 0, j, 0], CH), :] = (
             decoded * lax.rsqrt(jnp.sum(decoded * decoded, axis=-1, keepdims=True) + epsilon)
         ).astype(jnp.bfloat16)
-        spread(lambda *place: K_SLOT[place], j)
+        spread(j)
 
     acc[...] = jnp.zeros_like(acc)
     arrived(kord.at[pl.ds(1, 7)], o_sem.at[0])
-    for slot, (dz, dc, j) in enumerate(K_ORDER):
-        row = kord[dc * 4 + dz, j : j + 1, :]
-        kob[pl.ds(slot * CH, CH), :] = jnp.broadcast_to(row, (CH, CH)).T
+    for dz, dc, j in K_ORDER:
+        turned = jnp.broadcast_to(kord[dc * 4 + dz, j : j + 1, :], (CH, CH)).T
+        for h in range(2):
+            kob[pl.ds(K_ROW[dz, dc, j, h], HALF), :] = turned[h * HALF : (h + 1) * HALF]
     arrived(qord.at[pl.ds(1, 15)], o_sem.at[1])
 
     def tile(key_row, n_keys, block, n_blocks):
@@ -234,6 +244,11 @@
             best = jnp.max(part.reshape(n_keys // 8, 8, CH), axis=0)
             acc[block + h] = jnp.maximum(acc[block + h], best)
 
+    def tiles(*items):
+        scores = [tile(*item) for item in items]
+        for item, found in zip(items, scores):
+            keep(*item, found)
+
     def work(count, place, n_keys, n_blocks, together):
         def some(first, size):
             at = [place(first + i) for i in range(size)]
@@ -254,44 +269,51 @@
             n_kt * n_qt, lambda i: ((i % n_kt) * 4 * CH, (qt + i // n_kt) * 2), 4 * CH, 2, 2
         )
 
-    def new_keys(kt, n_qt):
-        work(n_qt // 2, lambda i: (kt * 4 * CH, i * 4), 4 * CH, 4, 1)
+    def new_keys(row, n_keys, n_qt):
+        work(n_qt // 2, lambda i: (row, i * 4), n_keys, 4, 1)
         if n_qt % 2:
-            work(1, lambda i: (kt * 4 * CH, (n_qt - 1) * 2), 4 * CH, 2, 1)
-
-    def other_core(place):
+            work(1, lambda i: (row, (n_qt - 1) * 2), n_keys, 2, 1)
+
+    def other_core(place, h=None):
         dz, _, j = place
-        slot = K_SLOT[dz, 1, j]
-        send(k_at(K_SLOT[place]), k_at(slot), k_sem.at[slot], device(dc=1))
-
-    def got_keys(*places):
+        send(k_part(place, h)[0], *k_part((dz, 1, j), h), device(dc=1))
+
+    def got_keys(*places, h=None):
         for place in places:
-            arrived(k_at(K_SLOT[place]), k_sem.at[K_SLOT[place]])
-
-    def got_queries(*places):
-        for place in places:
-            arrived(q_at(Q_SLOT[place]), q_sem.at[Q_SLOT[place]])
+            arrived(*k_part(place, h))
+
+    def got_queries(place, h):
+        arrived(*q_half(place, h))
 
     for tick in range(1, 7):
         if tick <= 4:
             j, dy = J_ORDER[tick - 1], DY_ORDER[tick - 1]
-            for ready in {1: (3,), 2: (1, 2)}.get(tick, ()):
-                got_queries((0, ready))
-                send_x(ready)
+            for ready in {1: (3, 1), 2: (2,)}.get(tick, ()):
+                for h in range(2):
+                    got_queries((0, ready), h)
+                    send_x(ready, h)
+            if tick == 1:
+                for h in range(2):
+                    send_y(2, h)
             got_keys((3, 0, j), (1, 0, j))
-            slot = K_SLOT[2, 0, j]
-            if j % 2 == 0:
-                send(k_at(K_SLOT[3, 0, j]), k_at(slot), k_sem.at[slot], device(dz=1))
+            side, to = ((3, 1), (1, 3))[j % 2]
+            if j < 2:
+                send(k_part((side, 0, j))[0], *k_part((2, 0, j)), device(dz=to))
             else:
-                send(k_at(K_SLOT[1, 0, j]), k_at(slot), k_sem.at[slot], device(dz=3))
+                for h in range(2):
+                    row = K_ROW[side, 0, j, h]
+                    send(kbuf.at[pl.ds(row, HALF), :], *k_part((2, 0, j), h), device(dz=to))
             other_core((3, 0, j))
             other_core((1, 0, j))
-            got_queries((3, dy), (1, dy))
-            slot = Q_SLOT[2, dy]
-            if dy in (0, 1):
-                send(q_at(Q_SLOT[3, dy]), q_at(slot), q_sem.at[slot], device(dx=1))
-            else:
-                send(q_at(Q_SLOT[1, dy]), q_at(slot), q_sem.at[slot], device(dx=3))
+            for h in range(2):
+                got_queries((3, dy), h)
+                got_queries((1, dy), h)
+            for passed in {2: (0, 3), 3: (1,), 4: (2,)}.get(tick, ()):
+                side, to = (3, 1) if passed in (0, 1) else (1, 3)
+                for h in range(2):
+                    send(
+                        q_half((side, passed), h)[0], *q_half((2, passed), h), device(dx=to)
+                    )
             if tick == 1:
                 got_keys(*((0, 1, own) for own in J_ORDER))
                 new_queries(0, 2, 2)
@@ -303,19 +325,36 @@
                 new_queries(tick + 1, 1, tick + 1)
                 n_q = tick + 2
             got_keys((3, 1, j), (1, 1, j))
-            new_keys(tick + 1, n_q)
+            new_keys((tick + 1) * 4 * CH, 4 * CH, n_q)
+        elif tick == 5:
+            got_keys((2, 0, 0), (2, 0, 1))
+            other_core((2, 0, 0))
+            other_core((2, 0, 1))
+            for dy in (0, 3):
+                for h in range(2):
+                    got_queries((2, dy), h)
+            tiles(*((kt * 4 * CH, 4 * CH, 12, 2) for kt in range(6)))
+            got_keys((2, 1, 0), (2, 1, 1))
+            tiles((6 * 4 * CH, 4 * CH, 0, 14))
         else:
-            j = 2 * (tick - 5)
-            got_queries(*Q_ORDER[2 * tick + 2 : 2 * tick + 4])
-            if tick == 6:
-                new_queries(7, 1, 7)
-            got_keys((2, 0, j), (2, 0, j + 1))
-            other_core((2, 0, j))
-            other_core((2, 0, j + 1))
-            if tick == 5:
-                new_queries(6, 1, 6)
-            got_keys((2, 1, j), (2, 1, j + 1))
-            new_keys(tick + 1, tick + 2)
+            last = 7 * 4 * CH
+            got_keys((2, 0, 2), (2, 0, 3), h=0)
+            other_core((2, 0, 2), 0)
+            other_core((2, 0, 3), 0)
+            got_keys((2, 1, 2), (2, 1, 3), h=0)
+            tiles((last, 2 * CH, 0, 14))
+            for dy in (1, 2):
+                for h in range(2):
+                    got_queries((2, dy), h)
+            tiles(*((kt * 4 * CH, 4 * CH, 14, 2) for kt in range(4)))
+            got_keys((2, 0, 2), (2, 0, 3), h=1)
+            other_core((2, 0, 2), 1)
+            other_core((2, 0, 3), 1)
+            tiles(
+                *((kt * 4 * CH, 4 * CH, 14, 2) for kt in range(4, 7)), (last, 2 * CH, 14, 2)
+            )
+            got_keys((2, 1, 2), (2, 1, 3), h=1)
+            tiles((last + 2 * CH, 2 * CH, 0, 16))
 
     for dx, dy in line:
         slot = Q_SLOT[(4 - dx) % 4, (4 - dy) % 4]
@@ -333,7 +372,7 @@
     low = answer - high - middle
     parts = jnp.concatenate([high, middle, low, jnp.zeros((13, 4 * CH), jnp.float32)], axis=0)
     back = jnp.dot(parts.astype(jnp.bfloat16), perm[...], preferred_element_type=jnp.float32)
-    out_ref[...] = back[0:1] + back[1:2] + back[2:3]
+    out_ref[...] = back[0:8]
     for copy in started:
         copy.wait_send()
 
@@ -344,7 +383,7 @@
     n_q, n_k = len(Q_ORDER), len(K_ORDER)
     out = pl.pallas_call(
         kernel,
-        out_shape=jax.ShapeDtypeStruct((1, n_rows), jnp.float32),
+        out_shape=jax.ShapeDtypeStruct((8, n_rows), jnp.float32),
         in_specs=[pl.BlockSpec(memory_space=pl.ANY)] * 8,
         out_specs=vmem,
         scratch_shapes=[
@@ -367,9 +406,9 @@
             pltpu.VMEM((n_q, 8, CH), jnp.float32),
             pltpu.VMEM((4 * CH, n_rows), jnp.bfloat16),
             pltpu.SemaphoreType.DMA((8,)),
-            pltpu.SemaphoreType.DMA((96,)),
-            pltpu.SemaphoreType.DMA((n_q,)),
-            pltpu.SemaphoreType.DMA((n_k,)),
+            pltpu.SemaphoreType.DMA((128,)),
+            pltpu.SemaphoreType.DMA((2 * n_q,)),
+            pltpu.SemaphoreType.DMA((2 * n_k,)),
             pltpu.SemaphoreType.DMA((3,)),
         ],
         compiler_params=pltpu.CompilerParams(
@@ -388,7 +427,7 @@
         counts,
         earlier_order,
     )
-    return out.reshape(n_rows)
+    return out[0] + out[1] + out[2]
 
 
 def solution(mesh):

time: 65.5 us -> 59.1 us (0.902)
  Pallas kernels: 64.1 us -> 57.6 us
  other arithmetic: 0 us -> 1.38 us
  local copies, waits for them, and re-layouts: 1.22 us -> 0 us
    pallas_call x1, Pallas kernels: 64.1 us -> 57.6 us  [per_device(): pl.pallas_call(kernel, out_shape=jax.ShapeDtypeStruct((8, n_rows), jnp.fl...]
    add x0 -> x1, other arithmetic: none -> 1.38 us  [per_device(): return out[0] + out[1] + out[2]]
    unnamed x3 -> x0, local copies, waits for them, and re-layouts: 1.22 us -> none
where the time goes in v3:
time: 59.1 us; the launch traced here: 59 us
  Pallas kernels  57.6 us (97%)
  other arithmetic  1.38 us (2%)
    pallas_call x1, Pallas kernels, per_device(): pl.pallas_call(kernel, out_shape=jax.ShapeDtypeStruct((8, n_rows), jnp.fl...  57.6 us
    add x1, other arithmetic, per_device(): return out[0] + out[1] + out[2]  1.38 us

profile of v3, /device:TPU:1, one launch (start us, length us, event | category | flops | bytes accessed | tf_op | source)
XLA Modules:
  0.0 59.0 jit_solution(5775773067334085186)
XLA Ops:
  0.0 57.6 %shard_map.82 = f32[8,256]{1,0:T(8,128)} custom-call(bf16[256,1024]{1,0:T(8,128)(2,1)} %rows_hbm.1, s32[1,256]{1,0:T(1,128)} %bitcast.5, s32[1,256]{1,0:T(1,128)} %bitcast.6, bf16[512,1024]{1,0:T(8,128)(2,1)} %bitcast.4, f32[2,1024]{1,0:T(2,128)} %scales_hbm.1, f32[2,1024]{1,0:T(2,128)} %offsets_hbm.1, s32[2]{0:T(128)} %counts_hbm.1, s32[2,256]{1,0:T(2,128)} %key_order_hbm.1), custom_call_target="tpu_custom_call" | custom-call | flops 17179869184 | bytes 2097152 | tf_op jit(solution)/shard_map/pallas_call | solution.py:384
  57.6 1.4 %slice_add_fusion = f32[1,256]{1,0:T(1,128)} fusion(f32[8,256]{1,0:T(8,128)} %shard_map.82), kind=kLoop, calls=%fused_computation | loop fusion | flops 512 | bytes 4096 | tf_op jit(solution)/shard_map/add | solution.py:430

commit v4 on v3

--- a/solution.py
+++ b/solution.py
@@ -45,8 +45,8 @@
     rows_hbm, ids_hbm, order_hbm, codes_hbm, scales_hbm, offsets_hbm, counts_hbm, key_order_hbm,
     out_ref,
     rows, ids_ref, order_ref, codes, scales_ref, offsets_ref, counts_ref, key_order_ref,
-    sendq, sendo, qbuf, kbuf, qord, kord, kob, acc, ans, perm,
-    local_sem, send_sem, q_sem, k_sem, o_sem,
+    sendq, sendo, qbuf, kbuf, qin, qord, kord, kob, acc, ans, perm,
+    local_sem, send_sem, q_sem, k_sem, qo_sem, ko_sem, back_sem,
 ):
     y = lax.axis_index("grp")
     shard = lax.axis_index("shard")
@@ -90,33 +90,76 @@
         row = K_ROW[place + (h or 0,)]
         return kbuf.at[pl.ds(row, CH if h is None else HALF), :], k_sem.at[row // HALF]
 
+    barrier = pltpu.get_barrier_semaphore()
+    near = [{"dx": 1}, {"dx": 3}, {"dy": 1}, {"dy": 2}, {"dy": 3}, {"dz": 1}, {"dz": 3}, {"dc": 1}]
+    for place in near:
+        pl.semaphore_signal(barrier, inc=1, device_id=device(**place), device_id_type=MESH)
+
+
     loads = [
         pltpu.make_async_copy(src, dst, local_sem.at[i])
         for i, (src, dst) in enumerate(
             (
+                (scales_hbm, scales_ref),
+                (offsets_hbm, offsets_ref),
+                (codes_hbm.at[pl.ds(0, CH), :], codes.at[pl.ds(0, CH), :]),
+                (counts_hbm, counts_ref),
+                (key_order_hbm, key_order_ref),
                 (ids_hbm, ids_ref),
                 (order_hbm, order_ref),
-                (counts_hbm, counts_ref),
-                (key_order_hbm, key_order_ref),
                 (rows_hbm, rows),
-                (scales_hbm, scales_ref),
-                (offsets_hbm, offsets_ref),
-                (codes_hbm, codes),
+                *((codes_hbm.at[pl.ds(j * CH, CH), :], codes.at[pl.ds(j * CH, CH), :]) for j in J_ORDER[1:]),
             )
         )
     ]
     for load in loads:
         load.start()
-    barrier = pltpu.get_barrier_semaphore()
-    line = [(dx, dy) for dx in range(4) for dy in range(4) if (dx, dy) != (0, 0)]
-    column = [(dz, dc) for dz in range(4) for dc in range(2) if (dz, dc) != (0, 0)]
-    for dx, dy in line:
-        pl.semaphore_signal(barrier, inc=1, device_id=device(dx=dx, dy=dy), device_id_type=MESH)
-    for dz, dc in column:
-        pl.semaphore_signal(barrier, inc=1, device_id=device(dz=dz, dc=dc), device_id_type=MESH)
+
+    def decode(i):
+        j = J_ORDER[i]
+        if i:
+            loads[7 + i].wait()
+        decoded = (
+            codes[pl.ds(j * CH, CH), :].astype(jnp.float32) * scales_ref[j // 2 : j // 2 + 1, :]
+            + offsets_ref[j // 2 : j // 2 + 1, :]
+        )
+        kbuf[pl.ds(K_ROW[0, 0, j, 0], CH), :] = (
+            decoded * lax.rsqrt(jnp.sum(decoded * decoded, axis=-1, keepdims=True) + epsilon)
+        ).astype(jnp.bfloat16)
+
+    def spread(j):
+        here, _ = k_part((0, 0, j))
+        for to, place in (
+            (device(dz=1), (3, 0, j)),
+            (device(dz=3), (1, 0, j)),
+            (device(dc=1), (0, 1, j)),
+        ):
+            send(here, *k_part(place), to)
+
+    def keys_order(dz, dc):
+        return kord.at[dc * 4 + dz], ko_sem.at[dc * 4 + dz]
+
+    for load in loads[:5]:
+        load.wait()
+    for j in range(4):
+        place = shard * 256 + (j % 2) * CH + lax.broadcasted_iota(jnp.int32, (1, CH), 1)
+        live = place < counts_ref[j // 2]
+        kord[0, j : j + 1, :] = jnp.where(
+            live, key_order_ref[j // 2 : j // 2 + 1, (j % 2) * CH : (j % 2 + 1) * CH], DEAD
+        )
+
+    decode(0)
+
+    pl.semaphore_wait(barrier, len(near))
+
+    here, _ = keys_order(0, 0)
+    send(here, *keys_order(3, 0), device(dz=1))
+    send(here, *keys_order(1, 0), device(dz=3))
+    send(here, *keys_order(0, 1), device(dc=1))
+    spread(J_ORDER[0])
 
     n_rows = rows.shape[0]
-    for load in loads[:4]:
+    for load in loads[5:7]:
         load.wait()
     ids = ids_ref[...]
     target = (ids // 2 - y + 4) % 4
@@ -150,17 +193,10 @@
             part = moved[4 * cluster : 4 * cluster + 4, d * CH : (d + 1) * CH]
             joined = part[0:1] + part[1:2] * 256 + part[2:3] * 65536 + part[3:4] * 16777216
             if d == 0:
-                qord[0, cluster : cluster + 1, :] = joined
+                qin[0, 0, cluster : cluster + 1, :] = joined
             else:
                 sendo[d, cluster : cluster + 1, :] = joined
-    for j in range(4):
-        place = shard * 256 + (j % 2) * CH + lax.broadcasted_iota(jnp.int32, (1, CH), 1)
-        live = place < counts_ref[j // 2]
-        kord[0, j : j + 1, :] = jnp.where(
-            live, key_order_ref[j // 2 : j // 2 + 1, (j % 2) * CH : (j % 2 + 1) * CH], DEAD
-        )
-
-    loads[4].wait()
+    loads[7].wait()
     values = rows[...].astype(jnp.float32)
     queries = (
         values * lax.rsqrt(jnp.sum(values * values, axis=-1, keepdims=True) + epsilon)
@@ -175,8 +211,6 @@
     for d in range(1, 4):
         sendq[d] = picked(d)
 
-    pl.semaphore_wait(barrier, len(line) + len(column))
-
     def send_x(dy, h):
         here, _ = q_half((0, dy), h)
         for dx, there in ((1, 3), (3, 1)):
@@ -185,48 +219,40 @@
     def send_y(d, h):
         send(sendq.at[d, pl.ds(h * HALF, HALF)], *q_half((0, (4 - d) % 4), h), device(dy=d))
 
-    for dz, dc in column:
-        slot = dc * 4 + (4 - dz) % 4
-        send(kord.at[0], kord.at[slot], o_sem.at[0], device(dz=dz, dc=dc))
-    for dx, dy in line:
-        slot = Q_SLOT[(4 - dx) % 4, (4 - dy) % 4]
-        source = sendo.at[dy] if dy else qord.at[0]
-        send(source, qord.at[slot], o_sem.at[1], device(dx=dx, dy=dy))
-
+    for d in range(1, 4):
+        send(sendo.at[d], qin.at[0, 4 - d], qo_sem.at[0], device(dy=d))
     for h in range(2):
         for d in (1, 3):
             send_y(d, h)
         send_x(0, h)
-
-    for load in loads[5:]:
-        load.wait()
-
-    def spread(j):
-        here, _ = k_part((0, 0, j))
-        for to, place in (
-            (device(dz=1), (3, 0, j)),
-            (device(dz=3), (1, 0, j)),
-            (device(dc=1), (0, 1, j)),
-        ):
-            send(here, *k_part(place), to)
-
-    for j in J_ORDER:
-        decoded = (
-            codes[pl.ds(j * CH, CH), :].astype(jnp.float32) * scales_ref[j // 2 : j // 2 + 1, :]
-            + offsets_ref[j // 2 : j // 2 + 1, :]
-        )
-        kbuf[pl.ds(K_ROW[0, 0, j, 0], CH), :] = (
-            decoded * lax.rsqrt(jnp.sum(decoded * decoded, axis=-1, keepdims=True) + epsilon)
-        ).astype(jnp.bfloat16)
-        spread(j)
+    for i in range(1, 4):
+        decode(i)
+        spread(J_ORDER[i])
+
+    arrived(qin.at[0, pl.ds(1, 3)], qo_sem.at[0])
+    send(qin.at[0], qin.at[3], qo_sem.at[3], device(dx=1))
+    send(qin.at[0], qin.at[1], qo_sem.at[1], device(dx=3))
+    for dz in (3, 1):
+        arrived(*keys_order(dz, 0))
+        send(keys_order(dz, 0)[0], *keys_order(dz, 1), device(dc=1))
+    send(keys_order(3, 0)[0], *keys_order(2, 0), device(dz=1))
+
+    def spread_orders(dz, dc):
+        for j in range(4):
+            turned = jnp.broadcast_to(kord[dc * 4 + dz, j : j + 1, :], (CH, CH)).T
+            for h in range(2):
+                kob[pl.ds(K_ROW[dz, dc, j, h], HALF), :] = turned[h * HALF : (h + 1) * HALF]
+
+    def place_orders(dx):
+        for dy in range(4):
+            qord[Q_SLOT[dx, dy]] = qin[dx, dy]
 
     acc[...] = jnp.zeros_like(acc)
-    arrived(kord.at[pl.ds(1, 7)], o_sem.at[0])
-    for dz, dc, j in K_ORDER:
-        turned = jnp.broadcast_to(kord[dc * 4 + dz, j : j + 1, :], (CH, CH)).T
-        for h in range(2):
-            kob[pl.ds(K_ROW[dz, dc, j, h], HALF), :] = turned[h * HALF : (h + 1) * HALF]
-    arrived(qord.at[pl.ds(1, 15)], o_sem.at[1])
+    place_orders(0)
+    for dz in (0, 3, 1):
+        spread_orders(dz, 0)
+        arrived(*keys_order(dz, 1))
+        spread_orders(dz, 1)
 
     def tile(key_row, n_keys, block, n_blocks):
         keys = kbuf[pl.ds(pl.multiple_of(key_row, 2 * CH), n_keys), :]
@@ -284,6 +310,11 @@
 
     def got_queries(place, h):
         arrived(*q_half(place, h))
+
+    def give_back(places):
+        for dx, dy in places:
+            slot = Q_SLOT[(4 - dx) % 4, (4 - dy) % 4]
+            send(acc.at[Q_SLOT[dx, dy]], ans.at[slot], back_sem.at[0], device(dx=dx, dy=dy))
 
     for tick in range(1, 7):
         if tick <= 4:
@@ -315,6 +346,10 @@
                         q_half((side, passed), h)[0], *q_half((2, passed), h), device(dx=to)
                     )
             if tick == 1:
+                for dx in (3, 1):
+                    arrived(qin.at[dx], qo_sem.at[dx])
+                    place_orders(dx)
+                send(qin.at[3], qin.at[2], qo_sem.at[2], device(dx=1))
                 got_keys(*((0, 1, own) for own in J_ORDER))
                 new_queries(0, 2, 2)
                 n_q = 2
@@ -325,7 +360,16 @@
                 new_queries(tick + 1, 1, tick + 1)
                 n_q = tick + 2
             got_keys((3, 1, j), (1, 1, j))
+            if tick == 4:
+                arrived(*keys_order(2, 0))
+                send(keys_order(2, 0)[0], *keys_order(2, 1), device(dc=1))
             new_keys((tick + 1) * 4 * CH, 4 * CH, n_q)
+            if tick == 4:
+                arrived(qin.at[2], qo_sem.at[2])
+                place_orders(2)
+                spread_orders(2, 0)
+                arrived(*keys_order(2, 1))
+                spread_orders(2, 1)
         elif tick == 5:
             got_keys((2, 0, 0), (2, 0, 1))
             other_core((2, 0, 0))
@@ -343,23 +387,22 @@
             other_core((2, 0, 3), 0)
             got_keys((2, 1, 2), (2, 1, 3), h=0)
             tiles((last, 2 * CH, 0, 14))
-            for dy in (1, 2):
-                for h in range(2):
-                    got_queries((2, dy), h)
-            tiles(*((kt * 4 * CH, 4 * CH, 14, 2) for kt in range(4)))
             got_keys((2, 0, 2), (2, 0, 3), h=1)
             other_core((2, 0, 2), 1)
             other_core((2, 0, 3), 1)
+            for dy in (1, 2):
+                for h in range(2):
+                    got_queries((2, dy), h)
             tiles(
-                *((kt * 4 * CH, 4 * CH, 14, 2) for kt in range(4, 7)), (last, 2 * CH, 14, 2)
+                *((kt * 4 * CH, 4 * CH, 14, 2) for kt in range(7)), (last, 2 * CH, 14, 2)
             )
             got_keys((2, 1, 2), (2, 1, 3), h=1)
-            tiles((last + 2 * CH, 2 * CH, 0, 16))
-
-    for dx, dy in line:
-        slot = Q_SLOT[(4 - dx) % 4, (4 - dy) % 4]
-        send(acc.at[Q_SLOT[dx, dy]], ans.at[slot], o_sem.at[2], device(dx=dx, dy=dy))
-    arrived(ans.at[pl.ds(1, 15)], o_sem.at[2])
+            tiles((last + 2 * CH, 2 * CH, 8, 8))
+            give_back(Q_ORDER[:7:-1])
+            tiles((last + 2 * CH, 2 * CH, 0, 8))
+            give_back(Q_ORDER[1:8])
+
+    arrived(ans.at[pl.ds(1, 15)], back_sem.at[0])
     answers = []
     for d in range(4):
         best = acc[0] if d == 0 else ans[Q_SLOT[0, d]]
@@ -399,17 +442,20 @@
             pltpu.VMEM((4, 2, CH), jnp.int32),
             pltpu.VMEM((n_q * CH, width), jnp.bfloat16),
             pltpu.VMEM((n_k * CH, width), jnp.bfloat16),
+            pltpu.VMEM((4, 4, 2, CH), jnp.int32),
             pltpu.VMEM((n_q, 2, CH), jnp.int32),
             pltpu.VMEM((8, 4, CH), jnp.int32),
             pltpu.VMEM((n_k * CH, CH), jnp.int32),
             pltpu.VMEM((n_q, 8, CH), jnp.float32),
             pltpu.VMEM((n_q, 8, CH), jnp.float32),
             pltpu.VMEM((4 * CH, n_rows), jnp.bfloat16),
-            pltpu.SemaphoreType.DMA((8,)),
+            pltpu.SemaphoreType.DMA((11,)),
             pltpu.SemaphoreType.DMA((128,)),
             pltpu.SemaphoreType.DMA((2 * n_q,)),
             pltpu.SemaphoreType.DMA((2 * n_k,)),
-            pltpu.SemaphoreType.DMA((3,)),
+            pltpu.SemaphoreType.DMA((4,)),
+            pltpu.SemaphoreType.DMA((8,)),
+            pltpu.SemaphoreType.DMA((1,)),
         ],
         compiler_params=pltpu.CompilerParams(
             collective_id=0, has_side_effects=True, vmem_limit_bytes=63 * 2**20

time: 59.1 us -> 58.1 us (0.983)
  Pallas kernels: 57.6 us -> 56.5 us
    pallas_call x1, Pallas kernels: 57.6 us -> 56.5 us  [per_device(): pl.pallas_call(kernel, out_shape=jax.ShapeDtypeStruct((8, n_rows), jnp.fl...]
where the time goes in v4:
time: 58.1 us; the launch traced here: 57.9 us
  Pallas kernels  56.5 us (97%)
  other arithmetic  1.38 us (2%)
    pallas_call x1, Pallas kernels, per_device(): pl.pallas_call(kernel, out_shape=jax.ShapeDtypeStruct((8, n_rows), jnp.fl...  56.5 us
    add x1, other arithmetic, per_device(): return out[0] + out[1] + out[2]  1.38 us

profile of v4, /device:TPU:1, one launch (start us, length us, event | category | flops | bytes accessed | tf_op | source)
XLA Modules:
  0.0 57.9 jit_solution(12324513923846090854)
XLA Ops:
  0.0 56.5 %shard_map.82 = f32[8,256]{1,0:T(8,128)} custom-call(bf16[256,1024]{1,0:T(8,128)(2,1)} %rows_hbm.1, s32[1,256]{1,0:T(1,128)} %bitcast.5, s32[1,256]{1,0:T(1,128)} %bitcast.6, bf16[512,1024]{1,0:T(8,128)(2,1)} %bitcast.4, f32[2,1024]{1,0:T(2,128)} %scales_hbm.1, f32[2,1024]{1,0:T(2,128)} %offsets_hbm.1, s32[2]{0:T(128)} %counts_hbm.1, s32[2,256]{1,0:T(2,128)} %key_order_hbm.1), custom_call_target="tpu_custom_call" | custom-call | flops 17179869184 | bytes 2097152 | tf_op jit(solution)/shard_map/pallas_call | solution.py:427
  56.5 1.4 %slice_add_fusion = f32[1,256]{1,0:T(1,128)} fusion(f32[8,256]{1,0:T(8,128)} %shard_map.82), kind=kLoop, calls=%fused_computation | loop fusion | flops 512 | bytes 4096 | tf_op jit(solution)/shard_map/add | solution.py:476

commit v5 on v4

--- a/solution.py
+++ b/solution.py
@@ -207,10 +207,6 @@
             perm[pl.ds(d * CH, CH), :], queries, preferred_element_type=jnp.float32
         ).astype(jnp.bfloat16)
 
-    qbuf[pl.ds(0, CH), :] = picked(0)
-    for d in range(1, 4):
-        sendq[d] = picked(d)
-
     def send_x(dy, h):
         here, _ = q_half((0, dy), h)
         for dx, there in ((1, 3), (3, 1)):
@@ -221,10 +217,14 @@
 
     for d in range(1, 4):
         send(sendo.at[d], qin.at[0, 4 - d], qo_sem.at[0], device(dy=d))
+    qbuf[pl.ds(0, CH), :] = picked(0)
+    for h in range(2):
+        send_x(0, h)
+    for d in (1, 3, 2):
+        sendq[d] = picked(d)
     for h in range(2):
         for d in (1, 3):
             send_y(d, h)
-        send_x(0, h)
     for i in range(1, 4):
         decode(i)
         spread(J_ORDER[i])
@@ -379,12 +379,13 @@
                     got_queries((2, dy), h)
             tiles(*((kt * 4 * CH, 4 * CH, 12, 2) for kt in range(6)))
             got_keys((2, 1, 0), (2, 1, 1))
-            tiles((6 * 4 * CH, 4 * CH, 0, 14))
-        else:
-            last = 7 * 4 * CH
+            tiles((6 * 4 * CH, 4 * CH, 0, 8))
             got_keys((2, 0, 2), (2, 0, 3), h=0)
             other_core((2, 0, 2), 0)
             other_core((2, 0, 3), 0)
+            tiles((6 * 4 * CH, 4 * CH, 8, 6))
+        else:
+            last = 7 * 4 * CH
             got_keys((2, 1, 2), (2, 1, 3), h=0)
             tiles((last, 2 * CH, 0, 14))
             got_keys((2, 0, 2), (2, 0, 3), h=1)
@@ -402,6 +403,8 @@
             tiles((last + 2 * CH, 2 * CH, 0, 8))
             give_back(Q_ORDER[1:8])
 
+    for copy in started[:-15]:
+        copy.wait_send()
     arrived(ans.at[pl.ds(1, 15)], back_sem.at[0])
     answers = []
     for d in range(4):
@@ -416,7 +419,7 @@
     parts = jnp.concatenate([high, middle, low, jnp.zeros((13, 4 * CH), jnp.float32)], axis=0)
     back = jnp.dot(parts.astype(jnp.bfloat16), perm[...], preferred_element_type=jnp.float32)
     out_ref[...] = back[0:8]
-    for copy in started:
+    for copy in started[-15:]:
         copy.wait_send()
 
 

time: 58.1 us -> 57.3 us (0.986)
  Pallas kernels: 56.5 us -> 55.7 us
    pallas_call x1, Pallas kernels: 56.5 us -> 55.7 us  [per_device(): pl.pallas_call(kernel, out_shape=jax.ShapeDtypeStruct((8, n_rows), jnp.fl...]
where the time goes in v5:
time: 57.3 us; the launch traced here: 57.1 us
  Pallas kernels  55.7 us (97%)
  other arithmetic  1.38 us (2%)
    pallas_call x1, Pallas kernels, per_device(): pl.pallas_call(kernel, out_shape=jax.ShapeDtypeStruct((8, n_rows), jnp.fl...  55.7 us
    add x1, other arithmetic, per_device(): return out[0] + out[1] + out[2]  1.38 us

profile of v5, /device:TPU:1, one launch (start us, length us, event | category | flops | bytes accessed | tf_op | source)
XLA Modules:
  0.0 57.1 jit_solution(6446384263744785969)
XLA Ops:
  0.0 55.7 %shard_map.82 = f32[8,256]{1,0:T(8,128)} custom-call(bf16[256,1024]{1,0:T(8,128)(2,1)} %rows_hbm.1, s32[1,256]{1,0:T(1,128)} %bitcast.5, s32[1,256]{1,0:T(1,128)} %bitcast.6, bf16[512,1024]{1,0:T(8,128)(2,1)} %bitcast.4, f32[2,1024]{1,0:T(2,128)} %scales_hbm.1, f32[2,1024]{1,0:T(2,128)} %offsets_hbm.1, s32[2]{0:T(128)} %counts_hbm.1, s32[2,256]{1,0:T(2,128)} %key_order_hbm.1), custom_call_target="tpu_custom_call" | custom-call | flops 17179869184 | bytes 2097152 | tf_op jit(solution)/shard_map/pallas_call | solution.py:430
  55.7 1.4 %slice_add_fusion = f32[1,256]{1,0:T(1,128)} fusion(f32[8,256]{1,0:T(8,128)} %shard_map.82), kind=kLoop, calls=%fused_computation | loop fusion | flops 512 | bytes 4096 | tf_op jit(solution)/shard_map/add | solution.py:479

commit v6 on v5

--- a/solution.py
+++ b/solution.py
@@ -220,11 +220,12 @@
     qbuf[pl.ds(0, CH), :] = picked(0)
     for h in range(2):
         send_x(0, h)
-    for d in (1, 3, 2):
+    for d in (1, 3):
         sendq[d] = picked(d)
     for h in range(2):
         for d in (1, 3):
             send_y(d, h)
+    sendq[2] = picked(2)
     for i in range(1, 4):
         decode(i)
         spread(J_ORDER[i])
@@ -312,17 +313,18 @@
         arrived(*q_half(place, h))
 
     def give_back(places):
-        for dx, dy in places:
+        for dx, dy in sorted(places, key=lambda p: -(min(p[0], 4 - p[0]) + min(p[1], 4 - p[1]))):
             slot = Q_SLOT[(4 - dx) % 4, (4 - dy) % 4]
             send(acc.at[Q_SLOT[dx, dy]], ans.at[slot], back_sem.at[0], device(dx=dx, dy=dy))
 
     for tick in range(1, 7):
         if tick <= 4:
             j, dy = J_ORDER[tick - 1], DY_ORDER[tick - 1]
-            for ready in {1: (3, 1), 2: (2,)}.get(tick, ()):
-                for h in range(2):
-                    got_queries((0, ready), h)
-                    send_x(ready, h)
+            if tick == 1:
+                for ready in (3, 1):
+                    for h in range(2):
+                        got_queries((0, ready), h)
+                        send_x(ready, h)
             if tick == 1:
                 for h in range(2):
                     send_y(2, h)
@@ -336,6 +338,10 @@
                     send(kbuf.at[pl.ds(row, HALF), :], *k_part((2, 0, j), h), device(dz=to))
             other_core((3, 0, j))
             other_core((1, 0, j))
+            if tick == 2:
+                for h in range(2):
+                    got_queries((0, 2), h)
+                    send_x(2, h)
             for h in range(2):
                 got_queries((3, dy), h)
                 got_queries((1, dy), h)

time: 57.3 us -> 57.2 us (level)
  no operation moved by 1% of the time
where the time goes in v6:
time: 57.2 us; the launch traced here: 57.1 us
  Pallas kernels  55.7 us (97%)
  other arithmetic  1.38 us (2%)
    pallas_call x1, Pallas kernels, per_device(): pl.pallas_call(kernel, out_shape=jax.ShapeDtypeStruct((8, n_rows), jnp.fl...  55.7 us
    add x1, other arithmetic, per_device(): return out[0] + out[1] + out[2]  1.38 us

profile of v6, /device:TPU:1, one launch (start us, length us, event | category | flops | bytes accessed | tf_op | source)
XLA Modules:
  0.0 57.1 jit_solution(14412220549999774850)
XLA Ops:
  0.0 55.7 %shard_map.82 = f32[8,256]{1,0:T(8,128)} custom-call(bf16[256,1024]{1,0:T(8,128)(2,1)} %rows_hbm.1, s32[1,256]{1,0:T(1,128)} %bitcast.5, s32[1,256]{1,0:T(1,128)} %bitcast.6, bf16[512,1024]{1,0:T(8,128)(2,1)} %bitcast.4, f32[2,1024]{1,0:T(2,128)} %scales_hbm.1, f32[2,1024]{1,0:T(2,128)} %offsets_hbm.1, s32[2]{0:T(128)} %counts_hbm.1, s32[2,256]{1,0:T(2,128)} %key_order_hbm.1), custom_call_target="tpu_custom_call" | custom-call | flops 17179869184 | bytes 2097152 | tf_op jit(solution)/shard_map/pallas_call | solution.py:436
  55.7 1.4 %slice_add_fusion = f32[1,256]{1,0:T(1,128)} fusion(f32[8,256]{1,0:T(8,128)} %shard_map.82), kind=kLoop, calls=%fused_computation | loop fusion | flops 512 | bytes 4096 | tf_op jit(solution)/shard_map/add | solution.py:485
